TPU v7x, 32 devices: a whole 2x2x4 slice. The times are simulated.
32 devices in a mesh: rad: 4 (over y, x), azi: 8 (over z, core).
Axes of the slice: x: 2, y: 2, z: 4, core: 2. Of those that a mesh axis runs over, the one named last changes fastest.
Arguments:
- fluid_state: float32 [32, 8, 16, 8192], P('rad', None, None, 'azi'), may hold values from -6 to 6
- orbit_shift: int32 [32], P('rad'), may hold values from 0 to 8191
- residual_speed: float32 [32], P('rad'), may hold values from -0.5 to 0.5
- coupling: float32 [8, 8], replicated, may hold values from -1.2 to 1.2
- radial_solve: float32 [8, 32, 32], replicated, as said below
Outputs:
- advanced: float32 [32, 8, 16, 8192], P('rad', None, None, 'azi')
Inputs may be any that keep to these rules, and one draw needn't show every extreme that they name: radial_solve is, for each field, a dense block of the inverse of the radial operator over the window's radii, whose entries fall off with the distance of the two radii.
All inputs are finite; a program needn't handle non-finite values.
Results may differ from a plain program's by a relative error of at most 0.0003.
Values sent between devices are 32-bit elements; how exact they have to be, the bound alone decides.
A program may use at most 128 MiB of HBM per device.

v0:
```python
import jax
import jax.numpy as jnp
from jax import lax
from jax.sharding import PartitionSpec as P


def with_halo(cells, sides, width, closed):
    for axis, dim in sides:
        count = lax.axis_size(axis)
        ends = count if closed else count - 1
        head = lax.slice_in_dim(cells, 0, width, axis=dim)
        tail = lax.slice_in_dim(cells, cells.shape[dim] - width, cells.shape[dim], axis=dim)
        cells = jnp.concatenate(
            [
                lax.ppermute(tail, axis, [(i, (i + 1) % count) for i in range(ends)]),
                cells,
                lax.ppermute(head, axis, [((i + 1) % count, i) for i in range(ends)]),
            ],
            axis=dim,
        )
    return cells


def from_behind(value, axis, steps):
    count = lax.axis_size(axis)
    pairs = [(source, (source + steps) % count) for source in range(count)]
    return lax.ppermute(value, axis, pairs)


def face_flux(left, right, speed):
    return 0.5 * speed * (left + right) - 0.5 * jnp.abs(speed) * (right - left)


def radial_term(advected, padded, coupling):
    return advected + jnp.einsum(
        "fg,rgzj->rfzj", coupling, padded[2:] - padded[:-2], precision=lax.Precision.HIGHEST
    )


def implicit_step(radial_solve, explicit):
    return jnp.einsum("frk,kfzj->rfzj", radial_solve, explicit, precision=lax.Precision.HIGHEST)


def band_rim(advected, coupling):
    padded = with_halo(advected, (("rad", 0),), 1, False)
    return radial_term(advected, padded, coupling)


def per_device(fluid_state, orbit_shift, residual_speed, coupling, radial_solve):
    rows, fields, planes, cells = fluid_state.shape
    blocks = lax.axis_size("azi")
    turns = orbit_shift // cells
    rest = orbit_shift % cells
    current = fluid_state
    power = 1
    while power < blocks:
        moved = from_behind(current, "azi", power)
        taken = turns // power % 2 == 1
        current = jnp.where(taken[:, None, None, None], moved, current)
        power = power * 2
    before = from_behind(current, "azi", 1)
    joined = jnp.concatenate([before, current], axis=3)

    def pick_row(row, start):
        return lax.dynamic_slice_in_dim(row, start, cells, axis=2)

    remapped = jax.vmap(pick_row)(joined, cells - rest)
    rimmed = with_halo(remapped, (("azi", 3),), 1, True)
    speed = residual_speed[:, None, None, None]
    lower = rimmed[:, :, :, :-2]
    upper = rimmed[:, :, :, 2:]
    advected = remapped - (face_flux(remapped, upper, speed) - face_flux(lower, remapped, speed))
    explicit = band_rim(advected, coupling)
    return lax.all_to_all(
        implicit_step(
            radial_solve, lax.all_to_all(explicit, "rad", split_axis=3, concat_axis=0, tiled=True)
        ),
        "rad",
        split_axis=0,
        concat_axis=3,
        tiled=True,
    )


def solution(mesh):
    return jax.shard_map(
        per_device,
        mesh=mesh,
        in_specs=(P("rad", None, None, "azi"), P("rad"), P("rad"), P(), P()),
        out_specs=P("rad", None, None, "azi"),
        check_vma=False,
    )
```

profile of v0, /device:TPU:0, one launch (start us, length us, event | category | flops | bytes accessed | tf_op | source)
XLA Modules:
  0.0 708.0 jit_solution(7901712423133402694)
XLA Ops:
  1.2 49.7 %collective-permute-done = f32[8,8,16,1024]{3,2,1,0:T(8,128)S(1)} collective-permute-done((f32[8,8,16,1024]{3,2,1,0:T(8,128)}, f32[8,8,16,1024]{3,2,1,0:T(8,128)S(1)}, u32[]{:S(2)}, u32[]{:S(2)}) %collective-permute-start) | collective-permute-done | bytes 4194336 | tf_op jit(solution)/shard_map/ppermute | solution.py:27
  50.9 3.2 broadcast_select_fusion
  54.4 92.0 %collective-permute-done.1 = f32[8,8,16,1024]{3,2,1,0:T(8,128)S(1)} collective-permute-done((f32[8,8,16,1024]{3,2,1,0:T(8,128)S(1)}, f32[8,8,16,1024]{3,2,1,0:T(8,128)S(1)}, u32[]{:S(2)}, u32[]{:S(2)}) %collective-permute-start.1) | collective-permute-done | bytes 4194336 | tf_op jit(solution)/shard_map/ppermute | solution.py:27
  148.7 179.6 %collective-permute-done.2 = f32[8,8,16,1024]{3,2,1,0:T(8,128)S(1)} collective-permute-done((f32[8,8,16,1024]{3,2,1,0:T(8,128)S(1)}, f32[8,8,16,1024]{3,2,1,0:T(8,128)S(1)}, u32[]{:S(2)}, u32[]{:S(2)}) %collective-permute-start.2) | collective-permute-done | bytes 4194336 | tf_op jit(solution)/shard_map/ppermute | solution.py:27
  328.3 3.0 broadcast_select_fusion.2
  331.3 50.0 %collective-permute-done.3 = f32[8,8,16,1024]{3,2,1,0:T(8,128)} collective-permute-done((f32[8,8,16,1024]{3,2,1,0:T(8,128)}, f32[8,8,16,1024]{3,2,1,0:T(8,128)}, u32[]{:S(2)}, u32[]{:S(2)}) %collective-permute-start.3) | collective-permute-done | bytes 4194336 | tf_op jit(solution)/shard_map/ppermute | solution.py:27
  381.3 7.8 %pad_maximum_fusion = f32[8,8,16,2048]{3,2,1,0:T(8,128)} fusion(f32[8,8,16,1024]{3,2,1,0:T(8,128)} %broadcast_select_fusion.2, f32[8,8,16,1024]{3,2,1,0:T(8,128)} %collective-permute-done.3), kind=kLoop, calls=%fused_computation.3 | loop fusion | flops 2097152 | bytes 16777216 | tf_op jit(solution)/shard_map/concatenate | solution.py:62
  389.1 34.6 %while.1 = (s32[]{:T(128)}, f32[8,8,16,2048]{3,2,1,0:T(8,128)}, s32[8,4]{0,1:T(4,128)S(1)}, f32[8,8,16,1024]{3,1,2,0:T(8,128)}, s32[]{:T(128)}) while((s32[]{:T(128)}, f32[8,8,16,2048]{3,2,1,0:T(8,128)}, s32[8,4]{0,1:T(4,128)S(1)}, f32[8,8,16,1024]{3,1,2,0:T(8,128)}, s32[]{:T(128)}) %tuple.24), condition=%wide.while_cond, body=%wide.while_body.sunk | while | flops 2 | bytes 2097785 | solution.py:65
  389.8 2.5 constant_dynamic-slice_fusion.5
  402.7 2.5 constant_dynamic-slice_fusion.5
  425.6 11.6 %collective-permute-done.4 = f32[8,8,16,1]{3,1,2,0:T(8,128)S(1)} collective-permute-done((f32[8,8,16,1]{3,1,2,0:T(8,128)S(1)}, f32[8,8,16,1]{3,1,2,0:T(8,128)S(1)}, u32[]{:S(2)}, u32[]{:S(2)}) %collective-permute-start.4) | collective-permute-done | bytes 4128 | tf_op jit(solution)/shard_map/ppermute | solution.py:17
  437.3 7.8 %fusion.10 = f32[8,8,16,1024]{3,1,2,0:T(8,128)S(1)} fusion(f32[8,8,16,1024]{3,1,2,0:T(8,128)} %get-tuple-element.12, f32[8,8,16,1]{3,1,2,0:T(8,128)S(1)} %collective-permute-done.5, f32[8,8,16,1]{3,1,2,0:T(8,128)S(1)} %collective-permute-done.4, f32[8]{0:T(128)S(1)} %get-tuple-element.30, f32[8]{0:T(128)S(1)} %get-tuple-element.29), kind=kLoop, calls=%fused_computation.16 | loop fusion | flops 14680064 | bytes 8396864 | tf_op jit(solution)/shard_map/sub | solution.py:72
  446.5 4.8 collective-permute-start.7
  451.3 10.6 %collective-permute-done.6 = f32[1,8,16,1024]{3,1,2,0:T(8,128)S(1)} collective-permute-done((f32[1,8,16,1024]{3,1,2,0:T(8,128)S(1)}, f32[1,8,16,1024]{3,1,2,0:T(8,128)S(1)}, u32[]{:S(2)}, u32[]{:S(2)}) %collective-permute-start.6) | collective-permute-done | bytes 524320 | tf_op jit(solution)/shard_map/ppermute | solution.py:17
  462.1 6.0 bitcast_add_fusion
  468.1 26.5 %copy.39 = f32[8,8,16,1024]{2,1,0,3:T(8,128)} copy(f32[8,8,16,1024]{3,1,2,0:T(8,128)} %bitcast_add_fusion) | data formatting | bytes 8388608 | tf_op jit(solution)/shard_map/add | solution.py:35
  494.6 29.4 %reshape.37 = f32[4,1,262144]{2,1,0:T(1,128)} reshape(f32[1024,8,8,16]{3,2,1,0:T(8,128)} %bitcast.37) | data formatting | bytes 8388608
  524.0 62.4 %all_to_all.36 = f32[4,1,262144]{2,1,0:T(1,128)} all-to-all(f32[4,1,262144]{2,1,0:T(1,128)} %reshape.37), channel_id=1, replica_groups=mesh['rad'=4,'azi'=8] {'rad'}, dimensions={0} | all-to-all | bytes 8388608 | tf_op jit(solution)/shard_map/all_to_all | solution.py:76
  587.0 15.5 %reduce = f32[4,262144]{1,0:T(4,128)} reduce(f32[4,1,262144]{2,1,0:T(1,128)} %all_to_all.36, f32[]{:T(128)} %broadcast.87), dimensions={1}, to_apply=%all_to_all.26.reduce_sub_computation | reduce | bytes 8388612 | tf_op jit(solution)/shard_map/all_to_all | solution.py:76
  602.6 24.9 %reshape.38 = f32[1024,8,8,16]{3,2,1,0:T(8,128)} reshape(f32[4,262144]{1,0:T(4,128)} %reduce) | data formatting | bytes 8388608
  627.5 21.1 %copy.40 = f32[8,8,16,4,256]{4,0,3,2,1:T(8,128)} copy(f32[8,8,16,4,256]{2,1,0,4,3:T(8,128)} %bitcast.38) | data formatting | bytes 8388608 | tf_op jit(solution)/shard_map/all_to_all | solution.py:76
  648.6 5.4 fusion.19
  656.4 48.9 %all_to_all.37 = f32[32,8,16,256]{3,2,1,0:T(8,128)S(1)} all-to-all(f32[32,8,16,256]{3,2,1,0:T(8,128)S(1)} %copy.41), channel_id=1, replica_groups=mesh['rad'=4,'azi'=8] {'rad'}, dimensions={0} | all-to-all | bytes 8388608 | tf_op jit(solution)/shard_map/all_to_all | solution.py:74
  705.3 2.7 copy.47
  (59 shorter events, 39.8 us)
Async XLA Ops:
  0.0 648.6 %copy-start = (f32[8,32,32]{2,1,0:T(8,128)S(1)}, f32[8,32,32]{2,1,0:T(8,128)}, u32[]{:S(2)}) copy-start(f32[8,32,32]{2,1,0:T(8,128)} %param.9) | copy-start | bytes 98308
  0.0 50.9 %collective-permute-start = (f32[8,8,16,1024]{3,2,1,0:T(8,128)}, f32[8,8,16,1024]{3,2,1,0:T(8,128)S(1)}, u32[]{:S(2)}, u32[]{:S(2)}) collective-permute-start(f32[8,8,16,1024]{3,2,1,0:T(8,128)} %param.5), channel_id=1, source_target_pairs={{0,1},{1,2},{2,3},{3,4},{4,5},{5,6},{6,7},{7,0},{8,9},{9,10},{10,1... | collective-permute-start | bytes 12582920 | tf_op jit(solution)/shard_map/ppermute | solution.py:27
  54.1 92.3 %collective-permute-start.1 = (f32[8,8,16,1024]{3,2,1,0:T(8,128)S(1)}, f32[8,8,16,1024]{3,2,1,0:T(8,128)S(1)}, u32[]{:S(2)}, u32[]{:S(2)}) collective-permute-start(f32[8,8,16,1024]{3,2,1,0:T(8,128)S(1)} %broadcast_select_fusion), channel_id=1, source_target_pairs={{0,2},{1,3},{2,4},{3,5},{4,6},{5,7},{6,0},{7,1},{8,10},{9,11},{10,... | collective-permute-start | bytes 12582920 | tf_op jit(solution)/shard_map/ppermute | solution.py:27
  147.8 180.4 %collective-permute-start.2 = (f32[8,8,16,1024]{3,2,1,0:T(8,128)S(1)}, f32[8,8,16,1024]{3,2,1,0:T(8,128)S(1)}, u32[]{:S(2)}, u32[]{:S(2)}) collective-permute-start(f32[8,8,16,1024]{3,2,1,0:T(8,128)S(1)} %broadcast_select_fusion.1), channel_id=1, source_target_pairs={{0,4},{1,5},{2,6},{3,7},{4,0},{5,1},{6,2},{7,3},{8,12},{9,13},{10,... | collective-permute-start | bytes 12582920 | tf_op jit(solution)/shard_map/ppermute | solution.py:27
  328.3 3.0 copy-start.2
  331.3 50.0 %collective-permute-start.3 = (f32[8,8,16,1024]{3,2,1,0:T(8,128)}, f32[8,8,16,1024]{3,2,1,0:T(8,128)}, u32[]{:S(2)}, u32[]{:S(2)}) collective-permute-start(f32[8,8,16,1024]{3,2,1,0:T(8,128)} %broadcast_select_fusion.2), channel_id=1, source_target_pairs={{0,1},{1,2},{2,3},{3,4},{4,5},{5,6},{6,7},{7,0},{8,9},{9,10},{10,1... | collective-permute-start | bytes 12582920 | tf_op jit(solution)/shard_map/ppermute | solution.py:27
  389.1 36.5 %copy-start.3 = (f32[8]{0:T(128)S(1)}, f32[8]{0:T(128)}, u32[]{:S(2)}) copy-start(f32[8]{0:T(128)} %param.7) | copy-start | bytes 100
  425.1 12.2 %collective-permute-start.4 = (f32[8,8,16,1]{3,1,2,0:T(8,128)S(1)}, f32[8,8,16,1]{3,1,2,0:T(8,128)S(1)}, u32[]{:S(2)}, u32[]{:S(2)}) collective-permute-start(f32[8,8,16,1]{3,1,2,0:T(8,128)S(1)} %get-tuple-element.27), channel_id=1, source_target_pairs={{1,0},{2,1},{3,2},{4,3},{5,4},{6,5},{7,6},{0,7},{9,8},{10,9},{11,1... | collective-permute-start | bytes 12296 | tf_op jit(solution)/shard_map/ppermute | solution.py:17
  425.1 12.1 %collective-permute-start.5 = (f32[8,8,16,1]{3,1,2,0:T(8,128)S(1)}, f32[8,8,16,1]{3,1,2,0:T(8,128)S(1)}, u32[]{:S(2)}, u32[]{:S(2)}) collective-permute-start(f32[8,8,16,1]{3,1,2,0:T(8,128)S(1)} %get-tuple-element.28), channel_id=1, source_target_pairs={{0,1},{1,2},{2,3},{3,4},{4,5},{5,6},{6,7},{7,0},{8,9},{9,10},{10,1... | collective-permute-start | bytes 12296 | tf_op jit(solution)/shard_map/ppermute | solution.py:15
  437.3 24.8 %copy-start.1 = (f32[8,8]{1,0:T(8,128)S(1)}, f32[8,8]{1,0:T(8,128)}, u32[]{:S(2)}) copy-start(f32[8,8]{1,0:T(8,128)} %param.8) | copy-start | bytes 772
  445.2 16.7 %collective-permute-start.6 = (f32[1,8,16,1024]{3,1,2,0:T(8,128)S(1)}, f32[1,8,16,1024]{3,1,2,0:T(8,128)S(1)}, u32[]{:S(2)}, u32[]{:S(2)}) collective-permute-start(f32[1,8,16,1024]{3,1,2,0:T(8,128)S(1)} %get-tuple-element.25), channel_id=1, source_target_pairs={{8,0},{16,8},{24,16},{9,1},{17,9},{25,17},{10,2},{18,10},{26,18},{... | collective-permute-start | bytes 1572872 | tf_op jit(solution)/shard_map/ppermute | solution.py:17
  446.5 15.5 %collective-permute-start.7 = (f32[1,8,16,1024]{3,1,2,0:T(8,128)S(1)}, f32[1,8,16,1024]{3,1,2,0:T(8,128)S(1)}, u32[]{:S(2)}, u32[]{:S(2)}) collective-permute-start(f32[1,8,16,1024]{3,1,2,0:T(8,128)S(1)} %get-tuple-element.26), channel_id=1, source_target_pairs={{0,8},{8,16},{16,24},{1,9},{9,17},{17,25},{2,10},{10,18},{18,26},{... | collective-permute-start | bytes 1572872 | tf_op jit(solution)/shard_map/ppermute | solution.py:15
where the time goes:
time: 709 us; the launch traced here: 708 us
  waiting for transfers between devices  394 us (56%)
  local copies, waits for them, and re-layouts  144 us (20%)
  blocking collectives  111 us (16%)
  other arithmetic  39.5 us (6%)
  matrix products  11.4 us (2%)
  starting transfers between devices  8.25 us (1%)
    ppermute x4, waiting for transfers between devices, from_behind(): return lax.ppermute(value, axis, pairs)  371 us
    all_to_all x1, blocking collectives, per_device(): lax.all_to_all(explicit, 'rad', split_axis=3, concat_axis=0, tiled=True)  62.4 us
    unnamed x11, local copies, waits for them, and re-layouts  54.3 us
    all_to_all x1, blocking collectives, per_device(): lax.all_to_all(implicit_step(radial_solve, lax.all_to_all(explicit, 'rad'...  48.9 us
    gather x32, local copies, waits for them, and re-layouts  34.5 us
    add x1, local copies, waits for them, and re-layouts, radial_term(): advected + jnp.einsum('fg,rgzj->rfzj', coupling, padded[2:] - padded[:-2]...  26.5 us
    ppermute x2, waiting for transfers between devices, with_halo(): lax.ppermute(head, axis, [((i + 1) % count, i) for i in range(ends)])  22.3 us
    all_to_all x2, local copies, waits for them, and re-layouts, per_device(): lax.all_to_all(explicit, 'rad', split_axis=3, concat_axis=0, tiled=True)  21.7 us
  transfers between devices with their start and end apart: 8, of which 7 were waited for; matrix products, arithmetic and copies ran while one was open for 0% of the time, Pallas kernels for 0%

commit v1 on v0

v1 whole, which is shorter than its diff:
```python
import jax
import jax.numpy as jnp
from jax import lax
from jax.sharding import PartitionSpec as P


def combined_matrix(coupling, radial_solve):
    fields, radii, _ = radial_solve.shape
    padded = jnp.pad(radial_solve, ((0, 0), (0, 0), (1, 1)))
    differences = padded[:, :, :-2] - padded[:, :, 2:]
    same = jnp.eye(fields, dtype=jnp.float32)
    solve = radial_solve.transpose(1, 0, 2)[:, :, :, None] * same[None, :, None, :]
    mixed = differences.transpose(1, 0, 2)[:, :, :, None] * coupling[None, :, None, :]
    return (solve + mixed).reshape(radii * fields, radii * fields)


def swap_in_plane(value, share):
    blocks = lax.axis_size("azi")
    groups = [list(range(first, first + share)) for first in range(0, blocks, share)]
    return lax.all_to_all(value, "azi", 0, 0, axis_index_groups=groups, tiled=True)


def per_device(fluid_state, orbit_shift, residual_speed, coupling, radial_solve):
    rows, fields, planes, cells = fluid_state.shape
    bands, blocks = lax.axis_size("rad"), lax.axis_size("azi")
    share = bands * blocks // planes
    per = rows // share
    part = lax.axis_index("azi") % share
    cycle = blocks * cells
    matrix = combined_matrix(coupling, radial_solve)
    shifts = lax.all_gather(orbit_shift, "rad").reshape(bands, share, per)
    speeds = lax.all_gather(residual_speed, "rad").reshape(bands, share, per)
    shifts = lax.dynamic_index_in_dim(shifts, part, 1, False).reshape(-1)
    speeds = lax.dynamic_index_in_dim(speeds, part, 1, False).reshape(-1)
    sent = fluid_state.transpose(2, 0, 1, 3).reshape(planes * share, per, fields, cells)
    got = lax.all_to_all(sent, ("rad", "azi"), 0, 0, tiled=True)
    got = got.reshape(bands, blocks, per, fields, cells).transpose(0, 2, 3, 1, 4)
    cyclic = got.reshape(bands * per, fields, cycle)
    wide = jnp.concatenate([cyclic[:, :, -1:], cyclic, cyclic, cyclic[:, :, :1]], axis=2)

    def pick_row(row, start):
        return lax.dynamic_slice_in_dim(row, start, cycle + 2, axis=1)

    rimmed = jax.vmap(pick_row)(wide, jnp.where(shifts == 0, 0, cycle - shifts))
    speed = speeds[:, None, None]
    size = jnp.abs(speed)
    advected = (
        (1.0 - size) * rimmed[:, :, 1:-1]
        + (0.5 * (size + speed)) * rimmed[:, :, :-2]
        + (0.5 * (size - speed)) * rimmed[:, :, 2:]
    )
    width = cycle // share
    halves = advected.reshape(bands, per, fields, share, width).transpose(3, 0, 1, 2, 4)
    halves = swap_in_plane(halves, share).transpose(1, 0, 2, 3, 4)
    columns = halves.reshape(bands * rows * fields, width)
    solved = jnp.dot(matrix, columns, precision=lax.Precision.HIGH)
    solved = solved.reshape(bands, share, per, fields, width).transpose(1, 0, 2, 3, 4)
    solved = swap_in_plane(solved, share).reshape(share, bands, per, fields, blocks // share, cells)
    back = solved.transpose(1, 0, 4, 2, 3, 5).reshape(bands * blocks, per, fields, cells)
    back = lax.all_to_all(back, ("rad", "azi"), 0, 0, tiled=True)
    return back.reshape(planes, rows, fields, cells).transpose(1, 2, 0, 3)


def solution(mesh):
    return jax.shard_map(
        per_device,
        mesh=mesh,
        in_specs=(P("rad", None, None, "azi"), P("rad"), P("rad"), P(), P()),
        out_specs=P("rad", None, None, "azi"),
        check_vma=False,
    )
```

time: 709 us -> 348 us (0.49)
  waiting for transfers between devices: 394 us -> 49.7 us
  blocking collectives: 111 us -> 147 us
  other arithmetic: 39.5 us -> 13.2 us
  local copies, waits for them, and re-layouts: 144 us -> 125 us
  matrix products: 11.4 us -> 2.06 us
    ppermute x8 -> x0, waiting for transfers between devices: 394 us -> none  [the longest x4 371 us: from_behind(): return lax.ppermute(value, axis, pairs)]
    all_to_all x0 -> x1, waiting for transfers between devices: none -> 49.7 us  [per_device(): got = lax.all_to_all(sent, ('rad', 'azi'), 0, 0, tiled=True)]
    unnamed x11 -> x17, local copies, waits for them, and re-layouts: 54.3 us -> 7.66 us
    unnamed x0 -> x2, blocking collectives: none -> 34.8 us
    gather x32 -> x48, local copies, waits for them, and re-layouts: 34.5 us -> 59.2 us
    all_to_all x3 -> x0, local copies, waits for them, and re-layouts: 24.4 us -> none  [the longest x2 21.7 us: per_device(): lax.all_to_all(explicit, 'rad', split_axis=3, concat_axis=0, tiled=True)]
    add x1, local copies, waits for them, and re-layouts: 26.5 us -> 4.02 us  [combined_matrix(): return (solve + mixed).reshape(radii * fields, radii * fields)]
    transpose x1 -> x8, local copies, waits for them, and re-layouts: 2.43 us -> 22.4 us  [the longest x1 7.77 us: per_device(): got.reshape(bands, blocks, per, fields, cells).transpose(0, 2, 3, 1, 4)]
  transfers between devices with their start and end apart: 8 -> 1, of which waited for: 7 -> 1; matrix products, arithmetic and copies ran while one was open for 0% -> 3% of each run, Pallas kernels for 0% -> 0%
where the time goes in v1:
time: 348 us; the launch traced here: 346 us
  blocking collectives  147 us (42%)
  local copies, waits for them, and re-layouts  125 us (36%)
  waiting for transfers between devices  49.7 us (14%)
  other arithmetic  13.2 us (4%)
  starting transfers between devices  7.43 us (2%)
    all_to_all x1, blocking collectives, per_device(): back = lax.all_to_all(back, ('rad', 'azi'), 0, 0, tiled=True)  97 us
    gather x48, local copies, waits for them, and re-layouts  59.2 us
    all_to_all x1, waiting for transfers between devices, per_device(): got = lax.all_to_all(sent, ('rad', 'azi'), 0, 0, tiled=True)  49.7 us
    unnamed x2, blocking collectives  34.8 us
    all_to_all x2, blocking collectives, swap_in_plane(): lax.all_to_all(value, 'azi', 0, 0, axis_index_groups=groups, tiled=True)  15.3 us
    concatenate x1, local copies, waits for them, and re-layouts, per_device(): jnp.concatenate([cyclic[:, :, -1:], cyclic, cyclic, cyclic[:, :, :1]], ax...  13.4 us
    add x1, other arithmetic, per_device(): (1.0 - size) * rimmed[:, :, 1:-1] + 0.5 * (size + speed) * rimmed[:, :, :-2]  9.03 us
    transpose x1, local copies, waits for them, and re-layouts, per_device(): got.reshape(bands, blocks, per, fields, cells).transpose(0, 2, 3, 1, 4)  7.77 us
  transfers between devices with their start and end apart: 1, of which 1 were waited for; matrix products, arithmetic and copies ran while one was open for 3% of the time, Pallas kernels for 0%

profile of v1, /device:TPU:0, one launch (start us, length us, event | category | flops | bytes accessed | tf_op | source)
XLA Modules:
  0.0 345.8 jit_solution(17393942769382413115)
XLA Ops:
  0.0 6.6 %copy.31 = f32[8,8,16,1024]{3,1,0,2:T(8,128)} copy(f32[8,8,16,1024]{3,2,1,0:T(8,128)} %param.5) | data formatting | bytes 8388608 | tf_op args[0]
  6.6 7.4 %all-to-all-start = ((f32[32,4,8,1024]{3,2,1,0:T(8,128)}), f32[32,4,8,1024]{3,2,1,0:T(8,128)}, u32[]{:S(2)}, u32[]{:S(2)}) async-start(f32[32,4,8,1024]{3,2,1,0:T(8,128)} %bitcast.38), calls=%async_computation | async-start | bytes 8388608 | tf_op jit(solution)/shard_map/all_to_all | solution.py:36
  15.7 27.0 %all-reduce.5 = s32[4,2,4]{2,1,0:T(2,128)S(1)} all-reduce(s32[4,2,4]{2,1,0:T(2,128)S(1)} %reshape.159), channel_id=3, replica_groups=mesh['rad'=4,'azi'=8] {'rad'}, use_global_device_ids=true, to_apply=%add.3 | all-reduce | flops 32 | bytes 256
  43.1 7.8 %all-reduce.4 = f32[4,2,4]{2,1,0:T(2,128)S(1)} all-reduce(f32[4,2,4]{2,1,0:T(2,128)S(1)} %reshape.155), channel_id=2, replica_groups=mesh['rad'=4,'azi'=8] {'rad'}, use_global_device_ids=true, to_apply=%add.2 | all-reduce | flops 32 | bytes 256
  51.4 4.0 %multiply_add_fusion.1 = f32[32,8,32,8]{3,2,1,0:T(8,128)} fusion(f32[8,8]{1,0:T(8,128)S(1)} %copy-done.1, f32[32,8,32]{2,1,0:T(8,128)S(1)} %copy.30, f32[8,8]{1,0:T(8,128)S(1)} %fusion, f32[32,8,32]{2,1,0:T(8,128)S(1)} %copy.29), kind=kLoop, calls=%fused_computation.4 | loop fusion | flops 196608 | bytes 328192 | tf_op jit(solution)/shard_map/add | solution.py:14
  55.3 4.0 %add.53 = f32[4,2,4,8,256]{4,3,2,1,0:T(8,128)S(1)} reshape(f32[32,8,32,8]{3,2,1,0:T(8,128)} %multiply_add_fusion.1) | data formatting | bytes 524288 | tf_op jit(solution)/shard_map/add | solution.py:14
  59.4 49.7 %all-to-all-done = f32[32,4,8,1024]{3,2,1,0:T(8,128)} async-done(((f32[32,4,8,1024]{3,2,1,0:T(8,128)}), f32[32,4,8,1024]{3,2,1,0:T(8,128)}, u32[]{:S(2)}, u32[]{:S(2)}) %all-to-all-start) | async-done | bytes 4194336 | tf_op jit(solution)/shard_map/all_to_all | solution.py:36
  109.1 7.8 %copy.32 = f32[4,4,8,8,1024]{4,3,2,1,0:T(8,128)} copy(f32[4,4,8,8,1024]{4,2,1,3,0:T(8,128)} %bitcast.6) | data formatting | bytes 8388608 | tf_op jit(solution)/shard_map/transpose | solution.py:37
  116.9 4.9 %reshape.158 = f32[16,8,8192]{2,1,0:T(8,128)} reshape(f32[4,4,8,8,1024]{4,3,2,1,0:T(8,128)} %copy.32) | data formatting | bytes 8388608 | tf_op jit(solution)/shard_map/reshape | solution.py:38
  122.8 13.4 %concatenate.6 = f32[16,8,16386]{2,1,0:T(8,128)} concatenate(f32[16,8,1]{2,1,0:T(8,128)S(1)} %get-tuple-element.24, f32[16,8,8192]{2,1,0:T(8,128)} %reshape.158, f32[16,8,8192]{2,1,0:T(8,128)} %reshape.158, f32[16,8,1]{2,1,0:T(8,128)S(1)} %get-tuple-element.23), dimensions={2} | concatenate | bytes 16779264 | tf_op jit(solution)/shard_map/concatenate | solution.py:39
  136.1 59.2 %while.1 = (s32[]{:T(128)}, f32[16,8,16386]{2,1,0:T(8,128)}, s32[16,3]{0,1:T(4,128)S(1)}, f32[16,8,8194]{2,1,0:T(8,128)}, s32[]{:T(128)}) while((s32[]{:T(128)}, f32[16,8,16386]{2,1,0:T(8,128)}, s32[16,3]{0,1:T(4,128)S(1)}, f32[16,8,8194]{2,1,0:T(8,128)}, s32[]{:T(128)}) %tuple.22), condition=%wide.while_cond, body=%wide.while_body.sunk | while | flops 2 | bytes 534121 | solution.py:42
  136.8 3.1 dynamic-slice_dynamic-update-slice_fusion.2
  140.5 3.1 dynamic-slice_dynamic-update-slice_fusion.2
  144.2 3.1 dynamic-slice_dynamic-update-slice_fusion.2
  170.1 3.1 dynamic-slice_dynamic-update-slice_fusion.2
  195.3 9.0 %multiply_add_fusion = f32[16,8,8192]{2,1,0:T(8,128)} fusion(f32[16,8,8194]{2,1,0:T(8,128)} %get-tuple-element.12, f32[16]{0:T(128)S(1)} %get-tuple-element.26, f32[16]{0:T(128)S(1)} %get-tuple-element.27, f32[16]{0:T(128)S(1)} %get-tuple-element.25), kind=kLoop, calls=%fused_computation.3 | loop fusion | flops 5242880 | bytes 16777408 | tf_op jit(solution)/shard_map/add | solution.py:48
  204.4 6.6 %reshape.160 = f32[4,4,8,2,4096]{4,3,2,1,0:T(2,128)} reshape(f32[16,8,8192]{2,1,0:T(8,128)} %multiply_add_fusion) | data formatting | bytes 8388608 | tf_op jit(solution)/shard_map/reshape | solution.py:53
  210.9 4.6 %copy.33 = f32[2,4,4,8,4096]{4,3,2,1,0:T(8,128)S(1)} copy(f32[2,4,4,8,4096]{4,0,3,2,1:T(2,128)} %bitcast.40) | data formatting | bytes 8388608 | tf_op jit(solution)/shard_map/transpose | solution.py:53
  215.6 7.1 %all_to_all.20 = f32[2,4,4,8,4096]{4,3,2,1,0:T(8,128)S(1)} all-to-all(f32[2,4,4,8,4096]{4,3,2,1,0:T(8,128)S(1)} %copy.33), channel_id=1, replica_groups={{0,1},{2,3},{4,5},{6,7},{8,9},{10,11},{12,13},{14,15},{16,17},{18,19},{..., dimensions={0} | all-to-all | bytes 8388608 | tf_op jit(solution)/shard_map/all_to_all | solution.py:20
  225.6 8.2 %all_to_all.21 = f32[2,4,4,8,4096]{4,3,2,1,0:T(8,128)} all-to-all(f32[2,4,4,8,4096]{4,3,2,1,0:T(8,128)S(1)} %copy.35), channel_id=1, replica_groups={{0,1},{2,3},{4,5},{6,7},{8,9},{10,11},{12,13},{14,15},{16,17},{18,19},{..., dimensions={0} | all-to-all | bytes 8388608 | tf_op jit(solution)/shard_map/all_to_all | solution.py:20
  233.8 6.0 %reshape.162 = f32[2,4,4,8,4,1024]{5,4,3,2,1,0:T(4,128)} reshape(f32[2,4,4,8,4096]{4,3,2,1,0:T(8,128)} %all_to_all.21) | data formatting | bytes 8388608 | tf_op jit(solution)/shard_map/reshape | solution.py:58
  239.8 4.6 %copy.36 = f32[4,2,4,4,8,1024]{5,4,3,2,1,0:T(8,128)S(1)} copy(f32[4,2,4,4,8,1024]{5,2,4,3,0,1:T(4,128)} %bitcast.42) | data formatting | bytes 8388608 | tf_op jit(solution)/shard_map/transpose | solution.py:59
  244.4 97.0 %all_to_all.22 = f32[32,4,8,1024]{3,2,1,0:T(8,128)S(1)} all-to-all(f32[32,4,8,1024]{3,2,1,0:T(8,128)S(1)} %bitcast.43), channel_id=1, replica_groups=mesh['rad'=4,'azi'=8] {'rad','azi'}, dimensions={0} | all-to-all | bytes 8388608 | tf_op jit(solution)/shard_map/all_to_all | solution.py:60
  341.4 4.4 %copy.37 = f32[8,8,16,1024]{3,2,1,0:T(8,128)} copy(f32[8,8,16,1024]{3,1,0,2:T(8,128)S(1)} %bitcast.44) | data formatting | bytes 8388608 | tf_op jit(solution)/shard_map/transpose | solution.py:61
  (78 shorter events, 52.4 us)
Async XLA Ops:
  6.6 7.5 %copy-start.4 = (u32[32]{0:T(128)S(1)}, u32[32]{0:T(128)}, u32[]{:S(2)}) copy-start(u32[32]{0:T(128)} %constant.59) | copy-start | bytes 388
  6.6 8.8 %copy-start.2 = (s32[8]{0:T(128)S(1)}, s32[8]{0:T(128)}, u32[]{:S(2)}) copy-start(s32[8]{0:T(128)} %param.6) | copy-start | bytes 100
  6.6 36.2 %copy-start.3 = (f32[8]{0:T(128)S(1)}, f32[8]{0:T(128)}, u32[]{:S(2)}) copy-start(f32[8]{0:T(128)} %param.7) | copy-start | bytes 100
  6.6 44.4 %copy-start = (f32[8,32,32]{2,1,0:T(8,128)S(1)}, f32[8,32,32]{2,1,0:T(8,128)}, u32[]{:S(2)}) copy-start(f32[8,32,32]{2,1,0:T(8,128)} %param.9) | copy-start | bytes 98308
  6.6 44.7 %copy-start.1 = (f32[8,8]{1,0:T(8,128)S(1)}, f32[8,8]{1,0:T(8,128)}, u32[]{:S(2)}) copy-start(f32[8,8]{1,0:T(8,128)} %param.8) | copy-start | bytes 772
  6.6 102.5 %all-to-all-start = ((f32[32,4,8,1024]{3,2,1,0:T(8,128)}), f32[32,4,8,1024]{3,2,1,0:T(8,128)}, u32[]{:S(2)}, u32[]{:S(2)}) async-start(f32[32,4,8,1024]{3,2,1,0:T(8,128)} %bitcast.38), calls=%async_computation | async-start | bytes 8388608 | tf_op jit(solution)/shard_map/all_to_all | solution.py:36

commit v2 on v1

v2 whole, which is shorter than its diff:
```python
import functools

import jax
import jax.numpy as jnp
from jax import lax
from jax.experimental import pallas as pl
from jax.experimental.pallas import tpu as pltpu
from jax.sharding import PartitionSpec as P

MESH = pl.DeviceIdType.MESH
GROUP = 8


def combined_matrix(coupling, radial_solve):
    fields, radii, _ = radial_solve.shape
    padded = jnp.pad(radial_solve, ((0, 0), (0, 0), (1, 1)))
    differences = padded[:, :, :-2] - padded[:, :, 2:]
    same = jnp.eye(fields, dtype=jnp.float32)
    solve = radial_solve.transpose(1, 0, 2)[:, :, :, None] * same[None, :, None, :]
    mixed = differences.transpose(1, 0, 2)[:, :, :, None] * coupling[None, :, None, :]
    return (solve + mixed).reshape(radii * fields, radii * fields)


def split(value):
    high = value.astype(jnp.bfloat16)
    return high, (value - high.astype(jnp.float32)).astype(jnp.bfloat16)


def mul(left, right):
    return jnp.dot(left, right, preferred_element_type=jnp.float32)


def kernel(
    bands, blocks, x, shifts, speeds, matrix, out,
    staged, landed, shared, columns, solved, arrived,
    send1, recv1, send2, recv2, send3, recv3,
):
    rows, fields, planes, cells = x.shape
    count = bands * blocks
    share = count // planes
    per = rows // share
    radii = bands * rows
    cycle = blocks * cells
    width = cycle // share
    wide = blocks // share
    band, block = lax.axis_index("rad"), lax.axis_index("azi")
    me = band * blocks + block
    part = lax.rem(block, share)
    first = me - part
    plane = me // share

    def place(device):
        return (device // blocks, lax.rem(device, blocks))

    barrier = pltpu.get_barrier_semaphore()

    @pl.loop(1, count)
    def _(step):
        pl.semaphore_signal(
            barrier, inc=1, device_id=place(lax.rem(me + step, count)), device_id_type=MESH
        )

    pl.semaphore_wait(barrier, count - 1)

    for q in range(per):
        for h in range(share):
            for g in range(planes // GROUP):
                turned = jnp.swapaxes(x[h * per + q, :, g * GROUP : (g + 1) * GROUP, :], 0, 1)
                for z in range(GROUP):
                    staged[q, (g * GROUP + z) * share + h] = turned[z]

        @pl.loop(1, count)
        def _(step):
            to = lax.rem(me + step, count)
            pltpu.make_async_remote_copy(
                src_ref=staged.at[q, to], dst_ref=landed.at[q, me],
                send_sem=send1.at[q, to], recv_sem=recv1.at[q, me],
                device_id=place(to), device_id_type=MESH,
            ).start()

        pltpu.make_async_copy(staged.at[q, me], landed.at[q, me], recv1.at[q, me]).start()

    for q in range(per):

        @pl.loop(0, count)
        def _(source):
            pltpu.make_async_copy(
                landed.at[q, source], landed.at[q, source], recv1.at[q, source]
            ).wait()

        for a in range(bands):
            row = jnp.concatenate([landed[q, a * blocks + b] for b in range(blocks)], axis=1)
            amount = shifts[a, part * per + q]
            speed = speeds[a, part * per + q]
            size = jnp.abs(speed)
            row = pltpu.roll(row, amount, 1)
            moved = (
                (1.0 - size) * row
                + (0.5 * (size + speed)) * pltpu.roll(row, 1, 1)
                + (0.5 * (size - speed)) * pltpu.roll(row, cycle - 1, 1)
            )
            k = a * rows + part * per + q
            for h in range(share):
                shared[q, a, h] = moved[:, h * width : (h + 1) * width]

                @pl.when(h != part)
                def _():
                    pltpu.make_async_remote_copy(
                        src_ref=shared.at[q, a, h], dst_ref=columns.at[k],
                        send_sem=send2.at[q, a, h], recv_sem=recv2.at[k],
                        device_id=place(first + h), device_id_type=MESH,
                    ).start()

                @pl.when(h == part)
                def _():
                    pltpu.make_async_copy(shared.at[q, a, h], columns.at[k], recv2.at[k]).start()

    @pl.loop(0, radii)
    def _(k):
        pltpu.make_async_copy(columns.at[k], columns.at[k], recv2.at[k]).wait()

    high, low = split(matrix[...])
    for c in range(wide):
        top, rest = split(
            columns[:, :, c * cells : (c + 1) * cells].reshape(radii * fields, cells)
        )
        result = mul(high, top) + (mul(high, rest) + mul(low, top))
        solved[c] = result.reshape(radii, fields, cells)
        for a in range(bands):
            owner = a * blocks + part * wide + c
            piece = solved.at[c, pl.ds(a * rows, rows)]

            @pl.when(owner != me)
            def _():
                pltpu.make_async_remote_copy(
                    src_ref=piece, dst_ref=arrived.at[plane],
                    send_sem=send3.at[c, a], recv_sem=recv3.at[plane],
                    device_id=place(owner), device_id_type=MESH,
                ).start()

            @pl.when(owner == me)
            def _():
                pltpu.make_async_copy(piece, arrived.at[plane], recv3.at[plane]).start()

    for g in range(planes // GROUP):

        @pl.loop(g * GROUP, (g + 1) * GROUP)
        def _(p):
            pltpu.make_async_copy(arrived.at[p], arrived.at[p], recv3.at[p]).wait()

        for r in range(rows):
            out[r, :, g * GROUP : (g + 1) * GROUP, :] = jnp.swapaxes(
                arrived[g * GROUP : (g + 1) * GROUP, r], 0, 1
            )

    for q in range(per):

        @pl.loop(1, count)
        def _(step):
            to = lax.rem(me + step, count)
            pltpu.make_async_copy(staged.at[q, to], staged.at[q, to], send1.at[q, to]).wait()

        for a in range(bands):
            for h in range(share):

                @pl.when(h != part)
                def _():
                    pltpu.make_async_copy(
                        shared.at[q, a, h], shared.at[q, a, h], send2.at[q, a, h]
                    ).wait()

    for c in range(wide):
        for a in range(bands):
            piece = solved.at[c, pl.ds(a * rows, rows)]

            @pl.when(a * blocks + part * wide + c != me)
            def _():
                pltpu.make_async_copy(piece, piece, send3.at[c, a]).wait()


def per_device(fluid_state, orbit_shift, residual_speed, coupling, radial_solve):
    rows, fields, planes, cells = fluid_state.shape
    bands, blocks = lax.axis_size("rad"), lax.axis_size("azi")
    count = bands * blocks
    share = count // planes
    per = rows // share
    radii = bands * rows
    width = blocks * cells // share
    wide = blocks // share
    matrix = combined_matrix(coupling, radial_solve)
    shifts = lax.all_gather(orbit_shift, "rad")
    speeds = lax.all_gather(residual_speed, "rad")
    vmem = pl.BlockSpec(memory_space=pltpu.VMEM)
    smem = pl.BlockSpec(memory_space=pltpu.SMEM)
    dma = pltpu.SemaphoreType.DMA
    return pl.pallas_call(
        functools.partial(kernel, bands, blocks),
        out_shape=jax.ShapeDtypeStruct(fluid_state.shape, jnp.float32),
        in_specs=[vmem, smem, smem, vmem],
        out_specs=vmem,
        scratch_shapes=[
            pltpu.VMEM((per, count, fields, cells), jnp.float32),
            pltpu.VMEM((per, count, fields, cells), jnp.float32),
            pltpu.VMEM((per, bands, share, fields, width), jnp.float32),
            pltpu.VMEM((radii, fields, width), jnp.float32),
            pltpu.VMEM((wide, radii, fields, cells), jnp.float32),
            pltpu.VMEM((planes, rows, fields, cells), jnp.float32),
            dma((per, count)),
            dma((per, count)),
            dma((per, bands, share)),
            dma((radii,)),
            dma((wide, bands)),
            dma((planes,)),
        ],
        compiler_params=pltpu.CompilerParams(
            collective_id=0, has_side_effects=True, vmem_limit_bytes=56 * 2**20
        ),
        cost_estimate=pl.CostEstimate(
            flops=6 * (radii * fields) ** 2 * width,
            bytes_accessed=2 * fluid_state.size * 4,
            transcendentals=0,
        ),
    )(fluid_state, shifts, speeds, matrix)


def solution(mesh):
    return jax.shard_map(
        per_device,
        mesh=mesh,
        in_specs=(P("rad", None, None, "azi"), P("rad"), P("rad"), P(), P()),
        out_specs=P("rad", None, None, "azi"),
        check_vma=False,
    )
```

time: 348 us -> 248 us (0.71)
  the two profiles are of different devices: /device:TPU:0 before, /device:TPU:15 now
where the time goes in v2:
time: 248 us
  Pallas kernels  216 us (87%)
  local copies, waits for them, and re-layouts  14.8 us (6%)
  blocking collectives  11 us (4%)
  other arithmetic  5.6 us (2%)
    pallas_call x1, Pallas kernels, per_device(): pl.pallas_call(functools.partial(kernel, bands, blocks), out_shape=jax.Sh...  216 us
    unnamed x2, blocking collectives  11 us
    unnamed x6, local copies, waits for them, and re-layouts  7.73 us

profile of v2, /device:TPU:15, one launch (start us, length us, event | category | flops | bytes accessed | tf_op | source)
XLA Modules:
  0.0 248.0 jit_solution(11142494512471954865)
XLA Ops:
  0.0 1.2 dynamic-slice
  1.9 0.9 dynamic-update-slice.1
  2.8 6.1 %all-reduce.2 = f32[32]{0:T(128)S(1)} all-reduce(f32[32]{0:T(128)S(1)} %dynamic-update-slice.1), channel_id=3, replica_groups=mesh['rad'=4,'azi'=8] {'rad'}, use_global_device_ids=true, to_apply=%add.2 | all-reduce | flops 32 | bytes 256
  8.9 0.8 dynamic-update-slice
  9.7 4.9 %all-reduce.1 = s32[32]{0:T(128)S(1)} all-reduce(s32[32]{0:T(128)S(1)} %dynamic-update-slice), channel_id=2, replica_groups=mesh['rad'=4,'azi'=8] {'rad'}, use_global_device_ids=true, to_apply=%add.1 | all-reduce | flops 32 | bytes 256
  14.6 0.7 reshape.19.shifts
  15.3 0.7 reshape.20.speeds
  16.0 1.0 copy.8
  16.9 1.1 subtract_bitcast_fusion
  18.1 0.1 copy.9
  18.2 4.5 %multiply_add_fusion = f32[32,8,32,8]{3,2,1,0:T(8,128)} fusion(f32[8,8]{1,0:T(8,128)} %param.8, f32[32,8,32]{2,1,0:T(8,128)S(1)} %copy.9, f32[8,8]{1,0:T(8,128)S(1)} %fusion, f32[32,8,32]{2,1,0:T(8,128)S(1)} %copy.8), kind=kLoop, calls=%fused_computation | loop fusion | flops 196608 | bytes 328192 | tf_op jit(solution)/shard_map/add | solution.py:21
  22.6 4.7 %add.10.matrix = f32[256,256]{1,0:T(8,128)} reshape(f32[32,8,32,8]{3,2,1,0:T(8,128)} %multiply_add_fusion) | data formatting | bytes 524288 | tf_op jit(solution)/shard_map/add | solution.py:21
  27.3 215.9 %shard_map.55 = f32[8,8,16,1024]{3,2,1,0:T(8,128)} custom-call(f32[8,8,16,1024]{3,2,1,0:T(8,128)} %x.5, s32[4,8]{1,0:T(4,128)} %reshape.19.shifts, f32[4,8]{1,0:T(4,128)} %reshape.20.speeds, f32[256,256]{1,0:T(8,128)} %add.10.matrix), custom_call_target="tpu_custom_call" | custom-call | flops 1610612736 | bytes 8388608 | tf_op jit(solution)/shard_map/pallas_call | solution.py:196
  243.2 4.8 %copy.13 = f32[8,8,16,1024]{3,2,1,0:T(8,128)} copy(f32[8,8,16,1024]{3,2,1,0:T(8,128)} %shard_map.55) | data formatting | bytes 8388608
  (3 shorter events, 0.0 us)

commit v3 on v2

--- a/solution.py
+++ b/solution.py
@@ -11,14 +11,26 @@
 GROUP = 8
 
 
-def combined_matrix(coupling, radial_solve):
-    fields, radii, _ = radial_solve.shape
-    padded = jnp.pad(radial_solve, ((0, 0), (0, 0), (1, 1)))
-    differences = padded[:, :, :-2] - padded[:, :, 2:]
-    same = jnp.eye(fields, dtype=jnp.float32)
-    solve = radial_solve.transpose(1, 0, 2)[:, :, :, None] * same[None, :, None, :]
-    mixed = differences.transpose(1, 0, 2)[:, :, :, None] * coupling[None, :, None, :]
-    return (solve + mixed).reshape(radii * fields, radii * fields)
+def fill_matrix(coupling, solve, matrix):
+    fields, radii, _ = solve.shape
+    shape = (radii, radii * fields)
+    inner = lax.broadcasted_iota(jnp.int32, shape, 0)
+    lane = lax.broadcasted_iota(jnp.int32, shape, 1)
+    outer, field = lane // fields, lax.rem(lane, fields)
+    zero = jnp.zeros(shape, jnp.float32)
+    for f in range(fields):
+        weight = zero
+        for g in range(fields):
+            weight = jnp.where(field == g, coupling[f, g], weight)
+        spread = (
+            jnp.where((inner == outer) & (field == f), 1.0, zero)
+            + jnp.where(inner + 1 == outer, weight, zero)
+            - jnp.where(inner == outer + 1, weight, zero)
+        )
+        matrix[:, f, :] = jnp.dot(
+            solve[f], spread,
+            precision=lax.Precision.HIGHEST, preferred_element_type=jnp.float32,
+        )
 
 
 def split(value):
@@ -31,9 +43,9 @@
 
 
 def kernel(
-    bands, blocks, x, shifts, speeds, matrix, out,
-    staged, landed, shared, columns, solved, arrived,
-    send1, recv1, send2, recv2, send3, recv3,
+    bands, blocks, x, shift, speed_in, coupling, solve, arrived,
+    staged, landed, shared, columns, solved, matrix, shift_all, speed_all, shifts, speeds,
+    send1, recv1, send2, recv2, send3, recv3, send4, recv4, moved4,
 ):
     rows, fields, planes, cells = x.shape
     count = bands * blocks
@@ -62,6 +74,22 @@
 
     pl.semaphore_wait(barrier, count - 1)
 
+    lane = lax.broadcasted_iota(jnp.int32, shift_all.shape[1:], 1)
+    own_shift = jnp.zeros(lane.shape, jnp.int32)
+    own_speed = jnp.zeros(lane.shape, jnp.float32)
+    for r in range(rows):
+        own_shift = jnp.where(lane == r, shift[r], own_shift)
+        own_speed = jnp.where(lane == r, speed_in[r], own_speed)
+    shift_all[band] = own_shift
+    speed_all[band] = own_speed
+    for step in range(1, bands):
+        for kind, table in enumerate((shift_all, speed_all)):
+            pltpu.make_async_remote_copy(
+                src_ref=table.at[band], dst_ref=table.at[band],
+                send_sem=send4.at[kind, step], recv_sem=recv4.at[kind, band],
+                device_id=(lax.rem(band + step, bands), block), device_id_type=MESH,
+            ).start()
+
     for q in range(per):
         for h in range(share):
             for g in range(planes // GROUP):
@@ -80,6 +108,23 @@
 
         pltpu.make_async_copy(staged.at[q, me], landed.at[q, me], recv1.at[q, me]).start()
 
+    fill_matrix(coupling, solve, matrix)
+
+    for kind, table in enumerate((shift_all, speed_all)):
+        for step in range(1, bands):
+            other = lax.rem(band + step, bands)
+            pltpu.make_async_copy(table.at[other], table.at[other], recv4.at[kind, other]).wait()
+        for step in range(1, bands):
+            pltpu.make_async_copy(table.at[band], table.at[band], send4.at[kind, step]).wait()
+    copies = [
+        pltpu.make_async_copy(shift_all, shifts, moved4.at[0]),
+        pltpu.make_async_copy(speed_all, speeds, moved4.at[1]),
+    ]
+    for copy in copies:
+        copy.start()
+    for copy in copies:
+        copy.wait()
+
     for q in range(per):
 
         @pl.loop(0, count)
@@ -90,8 +135,8 @@
 
         for a in range(bands):
             row = jnp.concatenate([landed[q, a * blocks + b] for b in range(blocks)], axis=1)
-            amount = shifts[a, part * per + q]
-            speed = speeds[a, part * per + q]
+            amount = shifts[a, 0, part * per + q]
+            speed = speeds[a, 0, part * per + q]
             size = jnp.abs(speed)
             row = pltpu.roll(row, amount, 1)
             moved = (
@@ -119,7 +164,7 @@
     def _(k):
         pltpu.make_async_copy(columns.at[k], columns.at[k], recv2.at[k]).wait()
 
-    high, low = split(matrix[...])
+    high, low = split(matrix[...].reshape(radii * fields, radii * fields))
     for c in range(wide):
         top, rest = split(
             columns[:, :, c * cells : (c + 1) * cells].reshape(radii * fields, cells)
@@ -142,16 +187,9 @@
             def _():
                 pltpu.make_async_copy(piece, arrived.at[plane], recv3.at[plane]).start()
 
-    for g in range(planes // GROUP):
-
-        @pl.loop(g * GROUP, (g + 1) * GROUP)
-        def _(p):
-            pltpu.make_async_copy(arrived.at[p], arrived.at[p], recv3.at[p]).wait()
-
-        for r in range(rows):
-            out[r, :, g * GROUP : (g + 1) * GROUP, :] = jnp.swapaxes(
-                arrived[g * GROUP : (g + 1) * GROUP, r], 0, 1
-            )
+    @pl.loop(0, planes)
+    def _(p):
+        pltpu.make_async_copy(arrived.at[p], arrived.at[p], recv3.at[p]).wait()
 
     for q in range(per):
 
@@ -176,6 +214,11 @@
             @pl.when(a * blocks + part * wide + c != me)
             def _():
                 pltpu.make_async_copy(piece, piece, send3.at[c, a]).wait()
+
+
+def turn_planes(planar, out):
+    for r in range(out.shape[0]):
+        out[r] = jnp.swapaxes(planar[:, r], 0, 1)
 
 
 def per_device(fluid_state, orbit_shift, residual_speed, coupling, radial_solve):
@@ -187,30 +230,35 @@
     radii = bands * rows
     width = blocks * cells // share
     wide = blocks // share
-    matrix = combined_matrix(coupling, radial_solve)
-    shifts = lax.all_gather(orbit_shift, "rad")
-    speeds = lax.all_gather(residual_speed, "rad")
     vmem = pl.BlockSpec(memory_space=pltpu.VMEM)
     smem = pl.BlockSpec(memory_space=pltpu.SMEM)
     dma = pltpu.SemaphoreType.DMA
-    return pl.pallas_call(
+    size = radii * fields
+    planar = pl.pallas_call(
         functools.partial(kernel, bands, blocks),
-        out_shape=jax.ShapeDtypeStruct(fluid_state.shape, jnp.float32),
-        in_specs=[vmem, smem, smem, vmem],
-        out_specs=vmem,
+        out_shape=jax.ShapeDtypeStruct((planes, rows, fields, cells), jnp.float32),
+        in_specs=[vmem, smem, smem, smem, vmem],
+        out_specs=pl.BlockSpec(memory_space=pl.ANY),
         scratch_shapes=[
             pltpu.VMEM((per, count, fields, cells), jnp.float32),
             pltpu.VMEM((per, count, fields, cells), jnp.float32),
             pltpu.VMEM((per, bands, share, fields, width), jnp.float32),
             pltpu.VMEM((radii, fields, width), jnp.float32),
             pltpu.VMEM((wide, radii, fields, cells), jnp.float32),
-            pltpu.VMEM((planes, rows, fields, cells), jnp.float32),
+            pltpu.VMEM((radii, fields, size), jnp.float32),
+            pltpu.VMEM((bands, 8, 128), jnp.int32),
+            pltpu.VMEM((bands, 8, 128), jnp.float32),
+            pltpu.SMEM((bands, 8, 128), jnp.int32),
+            pltpu.SMEM((bands, 8, 128), jnp.float32),
             dma((per, count)),
             dma((per, count)),
             dma((per, bands, share)),
             dma((radii,)),
             dma((wide, bands)),
             dma((planes,)),
+            dma((2, bands)),
+            dma((2, bands)),
+            dma((2,)),
         ],
         compiler_params=pltpu.CompilerParams(
             collective_id=0, has_side_effects=True, vmem_limit_bytes=56 * 2**20
@@ -220,7 +268,15 @@
             bytes_accessed=2 * fluid_state.size * 4,
             transcendentals=0,
         ),
-    )(fluid_state, shifts, speeds, matrix)
+    )(fluid_state, orbit_shift, residual_speed, coupling, radial_solve)
+    some = 2
+    return pl.pallas_call(
+        turn_planes,
+        grid=(planes // GROUP, rows // some),
+        in_specs=[pl.BlockSpec((GROUP, some, fields, cells), lambda g, r: (g, r, 0, 0))],
+        out_specs=pl.BlockSpec((some, fields, GROUP, cells), lambda g, r: (r, 0, g, 0)),
+        out_shape=jax.ShapeDtypeStruct(fluid_state.shape, jnp.float32),
+    )(planar)
 
 
 def solution(mesh):

time: 248 us -> 216 us (0.87)
  local copies, waits for them, and re-layouts: 14.8 us -> 0 us
  blocking collectives: 11 us -> 0 us
  other arithmetic: 5.6 us -> 0 us
    unnamed x2 -> x0, blocking collectives: 11 us -> none
    unnamed x6 -> x0, local copies, waits for them, and re-layouts: 7.73 us -> none
    pallas_call x1, Pallas kernels: 216 us -> 208 us  [per_device(): pl.pallas_call(functools.partial(kernel, bands, blocks), out_shape=jax.Sh...]
    pallas_call x0 -> x1, Pallas kernels: none -> 6.87 us  [per_device(): pl.pallas_call(turn_planes, grid=(planes // GROUP, rows // some), in_spec...]
    add x1 -> x0, local copies, waits for them, and re-layouts: 4.66 us -> none  [combined_matrix(): return (solve + mixed).reshape(radii * fields, radii * fields)]
    add x1 -> x0, other arithmetic: 4.48 us -> none  [combined_matrix(): return (solve + mixed).reshape(radii * fields, radii * fields)]
where the time goes in v3:
time: 216 us; the launch traced here: 215 us
  Pallas kernels  215 us (100%)
    pallas_call x1, Pallas kernels, per_device(): pl.pallas_call(functools.partial(kernel, bands, blocks), out_shape=jax.Sh...  208 us
    pallas_call x1, Pallas kernels, per_device(): pl.pallas_call(turn_planes, grid=(planes // GROUP, rows // some), in_spec...  6.87 us

profile of v3, /device:TPU:15, one launch (start us, length us, event | category | flops | bytes accessed | tf_op | source)
XLA Modules:
  0.0 215.3 jit_solution(1277640944706665808)
XLA Ops:
  0.0 208.5 %shard_map.55.planar = f32[16,8,8,1024]{3,2,1,0:T(8,128)} custom-call(f32[8,8,16,1024]{3,2,1,0:T(8,128)} %x.1, s32[8]{0:T(128)} %shift.1, f32[8]{0:T(128)} %speed_in.1, f32[8,8]{1,0:T(8,128)} %coupling.1, f32[8,32,32]{2,1,0:T(8,128)} %solve.1), custom_call_target="tpu_custom_call" | custom-call | flops 1610612736 | bytes 8388608 | tf_op jit(solution)/shard_map/pallas_call | solution.py:237
  208.5 6.9 %shard_map.56 = f32[8,8,16,1024]{3,2,1,0:T(8,128)} custom-call(f32[16,8,8,1024]{3,2,1,0:T(8,128)} %shard_map.55.planar), custom_call_target="tpu_custom_call" | custom-call | tf_op jit(solution)/shard_map/pallas_call | solution.py:273

commit v4 on v3

--- a/solution.py
+++ b/solution.py
@@ -171,7 +171,8 @@
         )
         result = mul(high, top) + (mul(high, rest) + mul(low, top))
         solved[c] = result.reshape(radii, fields, cells)
-        for a in range(bands):
+        for step in range(bands):
+            a = lax.rem(band + step + 1, bands)
             owner = a * blocks + part * wide + c
             piece = solved.at[c, pl.ds(a * rows, rows)]
 

time: 216 us -> 208 us (0.963)
  Pallas kernels: 215 us -> 206 us
    pallas_call x1, Pallas kernels: 208 us -> 199 us  [per_device(): pl.pallas_call(functools.partial(kernel, bands, blocks), out_shape=jax.Sh...]
where the time goes in v4:
time: 208 us; the launch traced here: 206 us
  Pallas kernels  206 us (99%)
    pallas_call x1, Pallas kernels, per_device(): pl.pallas_call(functools.partial(kernel, bands, blocks), out_shape=jax.Sh...  199 us
    pallas_call x1, Pallas kernels, per_device(): pl.pallas_call(turn_planes, grid=(planes // GROUP, rows // some), in_spec...  6.87 us

profile of v4, /device:TPU:15, one launch (start us, length us, event | category | flops | bytes accessed | tf_op | source)
XLA Modules:
  0.0 205.5 jit_solution(18032203466774673049)
XLA Ops:
  0.0 198.7 %shard_map.55.planar = f32[16,8,8,1024]{3,2,1,0:T(8,128)} custom-call(f32[8,8,16,1024]{3,2,1,0:T(8,128)} %x.1, s32[8]{0:T(128)} %shift.1, f32[8]{0:T(128)} %speed_in.1, f32[8,8]{1,0:T(8,128)} %coupling.1, f32[8,32,32]{2,1,0:T(8,128)} %solve.1), custom_call_target="tpu_custom_call" | custom-call | flops 1610612736 | bytes 8388608 | tf_op jit(solution)/shard_map/pallas_call | solution.py:238
  198.7 6.9 %shard_map.56 = f32[8,8,16,1024]{3,2,1,0:T(8,128)} custom-call(f32[16,8,8,1024]{3,2,1,0:T(8,128)} %shard_map.55.planar), custom_call_target="tpu_custom_call" | custom-call | tf_op jit(solution)/shard_map/pallas_call | solution.py:274
